TPU v7x, 512 devices: a whole 4x4x16 slice. The times are simulated.
512 devices in a mesh: dp: 16 (over y, x), expert: 32 (over z, core).
Axes of the slice: x: 4, y: 4, z: 16, core: 2. Of those that a mesh axis runs over, the one named last changes fastest.
Arguments:
- tokens: bfloat16 [65536, 512], P(('dp', 'expert')), may hold values from -6 to 6
- cotangent: bfloat16 [65536, 512], P(('dp', 'expert')), may hold values from -0.29882812 to 0.29882812
- labels: int32 [65536, 1], P(('dp', 'expert')), may hold values from 0 to 63; in each aligned block of 128 rows (0 to 127, 128 to 255, ...) at most 4 rows name the same one
- placement: int32 [64], replicated, may hold values from 0 to 63, each once
- mass: float32 [65536], P(('dp', 'expert')), may hold values from 0.1 to 10
- w_head: float32 [512, 16], replicated, may hold values from -0.25 to 0.25
- w_up: bfloat16 [64, 512, 2048], P('expert', None, 'dp'), may hold values from -0.25 to 0.25
- w_down: bfloat16 [64, 2048, 512], P('expert', 'dp'), may hold values from -0.125 to 0.125
- up_moment: bfloat16 [64, 512, 2048], P('expert', None, 'dp'), may hold values from -2 to 2
- up_square: bfloat16 [64, 512, 2048], P('expert', None, 'dp'), may hold values from 0.0099487305 to 1
- down_moment: bfloat16 [64, 2048, 512], P('expert', 'dp'), may hold values from -2 to 2
- down_square: bfloat16 [64, 2048, 512], P('expert', 'dp'), may hold values from 0.0099487305 to 1
Outputs:
- fine_precip: float32 [65536, 16], P(('dp', 'expert'))
- up_next: bfloat16 [64, 512, 2048], P('expert', None, 'dp')
- down_next: bfloat16 [64, 2048, 512], P('expert', 'dp')
- up_moment_next: bfloat16 [64, 512, 2048], P('expert', None, 'dp')
- up_square_next: bfloat16 [64, 512, 2048], P('expert', None, 'dp')
- down_moment_next: bfloat16 [64, 2048, 512], P('expert', 'dp')
- down_square_next: bfloat16 [64, 2048, 512], P('expert', 'dp')
Inputs may be any that keep to these rules, and one draw needn't show every extreme that they name: `labels`: within each device's block of 128 rows no regime is named more than 4 times, and in every draw some regime is named exactly 4 times in some block; every regime is named somewhere. `placement`: each regime stands in exactly one expert slot.
All inputs are finite; a program needn't handle non-finite values.
Results may differ from a plain program's by a relative error of at most 0.0045.
Values may be sent and summed in bfloat16 or wider, within the bound.
A program may use at most 64 MiB of HBM per device.

v0:
```python
import jax
import jax.numpy as jnp
from jax import lax
from jax.sharding import PartitionSpec as P

CAP = 4


beta_first = 0.9
beta_second = 0.95
correct_first = 1.0 - 0.9**20
correct_second = 1.0 - 0.95**20
learn_rate = 0.002
adam_epsilon = 1e-08


def gelu_parts(pre):
    normal_cdf = 0.5 * (1.0 + lax.erf(pre * 0.7071067811865476))
    density = jnp.exp(-0.5 * pre * pre) * 0.3989422804014327
    return (pre * normal_cdf, normal_cdf + pre * density)


def adam_step(weight, first, second, grad):
    new_first = beta_first * first.astype(jnp.float32) + (1.0 - beta_first) * grad
    new_second = beta_second * second.astype(jnp.float32) + (1.0 - beta_second) * grad * grad
    update = new_first / correct_first / (jnp.sqrt(new_second / correct_second) + adam_epsilon)
    moved = weight.astype(jnp.float32) - learn_rate * update
    return (
        moved.astype(jnp.bfloat16),
        new_first.astype(jnp.bfloat16),
        new_second.astype(jnp.bfloat16),
    )


def route_slots(labels, placement, capacity, holders, local_count):
    experts = placement.shape[0]
    regimes = jnp.arange(experts, dtype=jnp.int32)
    owner = jnp.sum(jnp.where(placement[None, :] == regimes[:, None], regimes[None, :], 0), axis=1)
    chosen = labels[:, 0][:, None] == regimes[None, :]
    target = jnp.sum(jnp.where(chosen, owner[None, :], 0), axis=1)
    onehot = (target[:, None] == regimes[None, :]).astype(jnp.int32)
    earlier = jnp.cumsum(onehot, axis=0) - onehot
    position = jnp.sum(earlier * onehot, axis=1)
    lane_index = target % local_count * holders + target // local_count
    return lane_index * capacity + position


def fill_slots(values, slots, count):
    row_count = values.shape[0]
    source = (
        jnp.full((count,), row_count, jnp.int32)
        .at[slots]
        .set(jnp.arange(row_count, dtype=jnp.int32))
    )
    padded = jnp.concatenate([values, jnp.zeros((1, values.shape[1]), values.dtype)], axis=0)
    return jnp.take(padded, source, axis=0)


def expert_rows(rows_x, rows_grad, w_in, w_out):
    pre = jnp.einsum("krd,kdf->krf", rows_x, w_in, preferred_element_type=jnp.float32)
    value, slope = gelu_parts(pre)
    hidden = value.astype(jnp.bfloat16)
    back = jnp.einsum("krd,kfd->krf", rows_grad, w_out, preferred_element_type=jnp.float32)
    hidden_grad = (back * slope).astype(jnp.bfloat16)
    return (hidden, hidden_grad)


def outer_in(rows_x, hidden_grad):
    return jnp.einsum("krd,krf->kdf", rows_x, hidden_grad, preferred_element_type=jnp.float32)


def outer_out(hidden, rows_grad):
    return jnp.einsum("krf,krd->kfd", hidden, rows_grad, preferred_element_type=jnp.float32)


def local(
    tokens,
    cotangent,
    labels,
    placement,
    mass,
    w_head,
    w_up,
    w_down,
    up_moment,
    up_square,
    down_moment,
    down_square,
):
    capacity = CAP
    experts = placement.shape[0]
    width = tokens.shape[1]
    local_count = w_up.shape[0]
    holders = lax.axis_size("expert")
    slots = route_slots(labels, placement, capacity, holders, local_count)
    slot_count = experts * capacity
    recv_rows = holders * capacity
    send_x = fill_slots(tokens, slots, slot_count).reshape(local_count, holders, capacity, width)
    send_grad = fill_slots(cotangent, slots, slot_count).reshape(
        local_count, holders, capacity, width
    )
    recv_x, recv_grad = (
        lax.all_to_all(send_x, "expert", split_axis=1, concat_axis=1, tiled=True),
        lax.all_to_all(send_grad, "expert", split_axis=1, concat_axis=1, tiled=True),
    )
    recv_x = recv_x.reshape(local_count, recv_rows, width)
    recv_grad = recv_grad.reshape(local_count, recv_rows, width)
    piece_x = lax.all_gather(recv_x, "dp", axis=1, tiled=True)
    piece_grad = lax.all_gather(recv_grad, "dp", axis=1, tiled=True)
    hidden, hidden_grad = expert_rows(piece_x, piece_grad, w_up, w_down)
    grad_in = outer_in(piece_x, hidden_grad)
    grad_out = outer_out(hidden, piece_grad)
    absorb_hidden_all = jnp.swapaxes(hidden, 0, 1)
    hidden_all, grad_in, grad_out = (absorb_hidden_all, grad_in, grad_out)
    summed = lax.psum_scatter(
        jnp.einsum("rkf,kfd->rkd", hidden_all, w_down, preferred_element_type=jnp.float32).astype(
            jnp.bfloat16
        ),
        "dp",
        scatter_dimension=0,
        tiled=True,
    )
    outgoing = jnp.swapaxes(summed, 0, 1).reshape(local_count, holders, capacity, width)
    returned = lax.all_to_all(outgoing, "expert", split_axis=1, concat_axis=1, tiled=True)
    expert_out = jnp.take(returned.reshape(slot_count, width), slots, axis=0)
    field = tokens.astype(jnp.float32) + expert_out.astype(jnp.float32)
    logits = jnp.dot(
        field, w_head, precision=lax.Precision.HIGHEST, preferred_element_type=jnp.float32
    )
    positive = jax.nn.softplus(logits) + 0.1
    fine_precip = mass[:, None] * positive / jnp.sum(positive, axis=1, keepdims=True)
    up_next, up_moment_next, up_square_next = adam_step(w_up, up_moment, up_square, grad_in)
    down_next, down_moment_next, down_square_next = adam_step(
        w_down, down_moment, down_square, grad_out
    )
    return (
        fine_precip,
        up_next,
        down_next,
        up_moment_next,
        up_square_next,
        down_moment_next,
        down_square_next,
    )


def solution(mesh):
    placed = (
        P(("dp", "expert"), None),
        P(("dp", "expert"), None),
        P(("dp", "expert"), None),
        P(),
        P(("dp", "expert")),
        P(),
        P("expert", None, "dp"),
        P("expert", "dp", None),
        P("expert", None, "dp"),
        P("expert", None, "dp"),
        P("expert", "dp", None),
        P("expert", "dp", None),
    )
    return jax.shard_map(
        local,
        mesh=mesh,
        in_specs=placed,
        out_specs=(
            P(("dp", "expert"), None),
            P("expert", None, "dp"),
            P("expert", "dp", None),
            P("expert", None, "dp"),
            P("expert", None, "dp"),
            P("expert", "dp", None),
            P("expert", "dp", None),
        ),
        check_vma=False,
    )
```

profile of v0, /device:TPU:1, one launch (start us, length us, event | category | flops | bytes accessed | tf_op | source)
XLA Modules:
  0.0 303.4 jit_solution(4484119608090613356)
XLA Ops:
  7.2 0.0 copy-start
  7.2 0.0 all-gather.3.cloned.1.call-start
  7.2 0.8 select_reduce_fusion.2
  8.0 0.8 select_reduce_fusion.1
  8.8 0.1 fusion.28
  8.9 0.2 reduce_window_sum.11
  9.1 0.2 select_reduce_fusion
  9.3 1.0 scatter_custom_fusion
  10.3 0.9 concatenate.7
  11.3 0.9 concatenate.6
  12.2 1.2 gather_fusion.2
  13.3 1.2 gather_fusion.1
  14.5 0.0 copy-start.2
  14.5 0.1 broadcast_select_fusion
  14.6 0.1 reshape.141
  14.7 0.1 copy.29
  14.8 38.5 %all_to_all.15 = bf16[2,32,4,512]{3,2,0,1:T(4,128)(2,1)S(1)} all-to-all(bf16[2,32,4,512]{3,2,0,1:T(4,128)(2,1)S(1)} %copy.29), channel_id=1, replica_groups=mesh['dp'=16,'expert'=32] {'expert'}, dimensions={1} | all-to-all | bytes 524288 | tf_op jit(solution)/shard_map/all_to_all | solution.py:103
  53.3 0.1 copy.30
  53.4 0.8 reshape.142
  54.2 0.0 all-gather.3.cloned.1.call-update
  54.2 0.0 copy-start.1
  54.2 0.0 reduce-scatter.2.cloned.1.call-start
  54.3 58.6 %all-gather.3.cloned.1.call-done = bf16[2,2048,512]{2,1,0:T(8,128)(2,1)} async-done(((bf16[2,128,512]{2,1,0:T(8,128)(2,1)}), bf16[2,2048,512]{2,1,0:T(8,128)(2,1)}) %all-gather.3.cloned.1.call-update) | async-done | bytes 4194320 | tf_op jit(solution)/shard_map/all_gather | solution.py:108
  112.9 0.0 copy-done.2
  112.9 3.4 %fusion.46 = f32[2,2048,128]{2,1,0:T(8,128)S(1)} fusion(bf16[2,2048,512]{2,1,0:T(8,128)(2,1)} %all-gather.3.cloned.1.call-done, bf16[2,512,128]{2,1,0:T(8,128)(2,1)S(1)} %copy-done.2), kind=kOutput, calls=%fused_computation.89 | convolution fusion | flops 536870912 | bytes 6553600 | tf_op jit(solution)/shard_map/krd,kdf->krf/dot_general | solution.py:60
  116.4 0.0 copy-done.1
  116.4 3.2 %convert_bitcast_fusion = bf16[2048,2,512]{2,0,1:T(8,128)(2,1)} fusion(bf16[2,128,512]{2,1,0:T(8,128)(2,1)S(1)} %copy-done.1, f32[2,2048,128]{2,1,0:T(8,128)S(1)} %fusion.46), kind=kOutput, calls=%fused_computation.4 | convolution fusion | flops 541589504 | bytes 6553600 | tf_op jit(solution)/shard_map/rkf,kfd->rkd/dot_general | solution.py:116
  119.6 0.0 reduce-scatter.2.cloned.1.call-update
  119.6 0.0 all-gather.5.cloned.1.call-start
  119.6 0.1 reshape.145
  119.7 0.0 copy-start.5
  119.7 0.0 copy-start.6
  119.7 0.1 copy.33
  119.8 34.9 %all_to_all.16 = bf16[2,32,4,512]{3,2,0,1:T(4,128)(2,1)S(1)} all-to-all(bf16[2,32,4,512]{3,2,0,1:T(4,128)(2,1)S(1)} %copy.33), channel_id=1, replica_groups=mesh['dp'=16,'expert'=32] {'expert'}, dimensions={1} | all-to-all | bytes 524288 | tf_op jit(solution)/shard_map/all_to_all | solution.py:104
  154.8 0.1 copy.34
  154.9 0.8 reshape.146
  155.6 0.0 all-gather.5.cloned.1.call-update
  155.7 55.1 %reduce-scatter.2.cloned.1.call-done = bf16[128,2,512]{2,0,1:T(8,128)(2,1)} async-done(((bf16[2048,2,512]{2,0,1:T(8,128)(2,1)}), bf16[128,2,512]{2,0,1:T(8,128)(2,1)}) %reduce-scatter.2.cloned.1.call-update) | async-done | bytes 262160 | tf_op jit(solution)/shard_map/reduce_scatter | solution.py:115
  210.8 1.0 reshape.143
  211.8 0.8 copy.31
  212.6 14.6 %all-to-all-start.1 = ((bf16[2,32,4,512]{3,2,0,1:T(4,128)(2,1)}), bf16[2,32,4,512]{3,2,0,1:T(4,128)(2,1)S(1)}, u32[]{:S(2)}, u32[]{:S(2)}) async-start(bf16[2,32,4,512]{3,2,0,1:T(4,128)(2,1)} %copy.31), calls=%async_computation.2 | async-start | bytes 524288 | tf_op jit(solution)/shard_map/all_to_all | solution.py:124
  227.3 55.6 %all-gather.5.cloned.1.call-done = bf16[2,2048,512]{2,1,0:T(8,128)(2,1)} async-done(((bf16[2,128,512]{2,1,0:T(8,128)(2,1)}), bf16[2,2048,512]{2,1,0:T(8,128)(2,1)}) %all-gather.5.cloned.1.call-update) | async-done | bytes 4194320 | tf_op jit(solution)/shard_map/all_gather | solution.py:109
  282.9 0.0 copy-done.5
  282.9 0.0 copy-done.6
  282.9 4.4 %fusion.19 = (bf16[2,128,512]{2,1,0:T(8,128)(2,1)}, bf16[2,128,512]{2,1,0:T(8,128)(2,1)}, bf16[2,128,512]{2,1,0:T(8,128)(2,1)}) fusion(bf16[2,128,512]{2,1,0:T(8,128)(2,1)S(1)} %copy-done.5, bf16[2,128,512]{2,1,0:T(8,128)(2,1)S(1)} %copy-done.6, bf16[2,128,512]{2,1,0:T(8,128)(2,1)S(1)} %copy-done.1, bf16[2,2048,512]{2,1,0:T(8,128)(2,1)} %all-gather.5.cloned.1.call-done, ...), kind=kOutput, calls=%fused_computation.35 | convolution fusion | flops 541982720 | bytes 7864320 | tf_op jit(solution)/shard_map/krf,krd->kfd/dot_general | solution.py:73
  287.3 7.5 %fusion.20 = (bf16[2,512,128]{2,1,0:T(8,128)(2,1)}, bf16[2,512,128]{2,1,0:T(8,128)(2,1)}, bf16[2,512,128]{2,1,0:T(8,128)(2,1)}) fusion(bf16[2,512,128]{2,1,0:T(8,128)(2,1)} %param.23, bf16[2,512,128]{2,1,0:T(8,128)(2,1)} %param.22, bf16[2,512,128]{2,1,0:T(8,128)(2,1)S(1)} %copy-done.2, bf16[2,2048,512]{2,1,0:T(8,128)(2,1)} %all-gather.3.cloned.1.call-done, ...), kind=kOutput, calls=%fused_computation.36 | convolution fusion | flops 1081475072 | bytes 12320768 | tf_op jit(solution)/shard_map/krd,krf->kdf/dot_general | solution.py:69
  294.7 0.0 copy-start.3
  294.7 0.0 copy-start.4
  294.7 0.0 all-to-all-done.1
  294.7 0.1 copy.32
  294.8 0.1 reshape.144
  294.9 0.8 gather_fusion
  295.7 0.0 copy-done
  295.8 0.0 copy-done.3
  295.8 0.5 fusion.45
  296.2 0.0 copy-done.4
  296.2 0.6 multiply_divide_fusion
  (7 shorter events, 0.1 us)
Async XLA Ops:
  7.2 288.6 %copy-start = (f32[512,16]{0,1:T(8,128)S(1)}, f32[512,16]{0,1:T(8,128)}, u32[]{:S(2)}) copy-start(f32[512,16]{0,1:T(8,128)} %param.19) | copy-start | bytes 98308
  7.2 105.7 %all-gather.3.cloned.1.call-start = ((), (), s32[]{:S(2)}) async-start(), calls=%async_computation.4 | async-start | bytes 4456448 | tf_op jit(solution)/shard_map/all_gather | solution.py:108
  14.5 98.4 %copy-start.2 = (bf16[2,512,128]{2,1,0:T(8,128)(2,1)S(1)}, bf16[2,512,128]{2,1,0:T(8,128)(2,1)}, u32[]{:S(2)}) copy-start(bf16[2,512,128]{2,1,0:T(8,128)(2,1)} %param.20) | copy-start | bytes 786436
  54.2 62.1 %copy-start.1 = (bf16[2,128,512]{2,1,0:T(8,128)(2,1)S(1)}, bf16[2,128,512]{2,1,0:T(8,128)(2,1)}, u32[]{:S(2)}) copy-start(bf16[2,128,512]{2,1,0:T(8,128)(2,1)} %param.21) | copy-start | bytes 786436
  54.2 156.5 %reduce-scatter.2.cloned.1.call-start = ((), (), s32[]{:S(2)}) async-start(), calls=%async_computation.5 | async-start | bytes 4456448 | tf_op jit(solution)/shard_map/reduce_scatter | solution.py:115
  119.6 163.3 %all-gather.5.cloned.1.call-start = ((), (), s32[]{:S(2)}) async-start(), calls=%async_computation.6 | async-start | bytes 4456448 | tf_op jit(solution)/shard_map/all_gather | solution.py:109
  119.7 163.2 %copy-start.5 = (bf16[2,128,512]{2,1,0:T(8,128)(2,1)S(1)}, bf16[2,128,512]{2,1,0:T(8,128)(2,1)}, u32[]{:S(2)}) copy-start(bf16[2,128,512]{2,1,0:T(8,128)(2,1)} %param.25) | copy-start | bytes 786436
  119.7 163.2 %copy-start.6 = (bf16[2,128,512]{2,1,0:T(8,128)(2,1)S(1)}, bf16[2,128,512]{2,1,0:T(8,128)(2,1)}, u32[]{:S(2)}) copy-start(bf16[2,128,512]{2,1,0:T(8,128)(2,1)} %param.24) | copy-start | bytes 786436
  212.6 82.1 %all-to-all-start.1 = ((bf16[2,32,4,512]{3,2,0,1:T(4,128)(2,1)}), bf16[2,32,4,512]{3,2,0,1:T(4,128)(2,1)S(1)}, u32[]{:S(2)}, u32[]{:S(2)}) async-start(bf16[2,32,4,512]{3,2,0,1:T(4,128)(2,1)} %copy.31), calls=%async_computation.2 | async-start | bytes 524288 | tf_op jit(solution)/shard_map/all_to_all | solution.py:124
  294.7 1.0 copy-start.3
  294.7 1.5 copy-start.4
Sparse Core Ops, SparseCore 0:
  54.4 58.5 all-gather.2
  119.7 91.0 reduce-scatter.1
  214.8 68.0 all-gather.4
where the time goes:
time: 304 us; the launch traced here: 303 us
  waiting for transfers between devices  169 us (56%)
  blocking collectives  73.5 us (24%)
  matrix products  18.9 us (6%)
  starting transfers between devices  14.8 us (5%)
  between operations  14 us (5%)
  local copies, waits for them, and re-layouts  10 us (3%)
    all_gather x1, waiting for transfers between devices, local(): piece_x = lax.all_gather(recv_x, 'dp', axis=1, tiled=True)  58.6 us
    all_gather x1, waiting for transfers between devices, local(): piece_grad = lax.all_gather(recv_grad, 'dp', axis=1, tiled=True)  55.6 us
    reduce_scatter x1, waiting for transfers between devices, local(): lax.psum_scatter(jnp.einsum('rkf,kfd->rkd', hidden_all, w_down, preferred...  55.1 us
    all_to_all x1, blocking collectives, local(): lax.all_to_all(send_x, 'expert', split_axis=1, concat_axis=1, tiled=True)  38.5 us
    all_to_all x1, blocking collectives, local(): lax.all_to_all(send_grad, 'expert', split_axis=1, concat_axis=1, tiled=True)  34.9 us
    all_to_all x1, starting transfers between devices, local(): lax.all_to_all(outgoing, 'expert', split_axis=1, concat_axis=1, tiled=True)  14.6 us
    dot_general x1, matrix products, outer_in(): jnp.einsum('krd,krf->kdf', rows_x, hidden_grad, preferred_element_type=jn...  7.45 us
  transfers between devices with their start and end apart: 4, of which 3 were waited for; matrix products, arithmetic and copies ran while one was open for 5% of the time, Pallas kernels for 0%

commit v1 on v0

v1 whole, which is shorter than its diff:
```python
import functools

import jax
import jax.numpy as jnp
from jax import lax
from jax.experimental import pallas as pl
from jax.experimental.pallas import tpu as pltpu
from jax.sharding import PartitionSpec as P

MESH = pl.DeviceIdType.MESH
F32 = jnp.float32
BF16 = jnp.bfloat16

CAP = 4
NX = 4
NY = 4

beta_first = 0.9
beta_second = 0.95
correct_first = 1.0 - 0.9**20
correct_second = 1.0 - 0.95**20
learn_rate = 0.002
adam_epsilon = 1e-08


def gelu_parts(pre):
    normal_cdf = 0.5 * (1.0 + lax.erf(pre * 0.7071067811865476))
    density = jnp.exp(-0.5 * pre * pre) * 0.3989422804014327
    return (pre * normal_cdf, normal_cdf + pre * density)


def adam_step(weight, first, second, grad):
    new_first = beta_first * first.astype(F32) + (1.0 - beta_first) * grad
    new_second = beta_second * second.astype(F32) + (1.0 - beta_second) * grad * grad
    update = new_first / correct_first / (jnp.sqrt(new_second / correct_second) + adam_epsilon)
    moved = weight.astype(F32) - learn_rate * update
    return moved.astype(BF16), new_first.astype(BF16), new_second.astype(BF16)


def dot(a, b, contract=((1,), (0,))):
    return lax.dot_general(a, b, (contract, ((), ())), preferred_element_type=F32)


def kernel(
    nz,
    tok_ref, cot_ref, lab_ref, plc_ref, mass_ref, head_ref,
    wup_ref, wdn_ref, um_ref, us_ref, dm_ref, ds_ref,
    fine_ref, upn_ref, dnn_ref, umn_ref, usn_ref, dmn_ref, dsn_ref,
    st_ref, zsrc, zbuf, ysrc, xbuf, wup, wdn, hid, slope, hg, part, rsbuf,
    ysend, yret, zsend, zret, gs_up, gs_dn, gr_up, gr_dn, gy_up, gy_dn, gf_up, gf_dn,
    w_send, w_recv, z_send, z_recv, y_send, y_recv, x_send, x_recv,
    rs_send, rs_recv, g_send, g_recv, gy_send, gy_recv,
):
    dp = lax.axis_index("dp")
    ex = lax.axis_index("expert")
    y, x = dp // NX, dp % NX
    z, c = ex // 2, ex % 2
    tokens, width = tok_ref.shape
    group = wup_ref.shape[2]
    slots = nz * NY * CAP
    rows = nz * CAP
    chunk = NY * rows

    def at(yy=None, xx=None, zz=None, cc=None):
        yy = y if yy is None else yy
        xx = x if xx is None else xx
        zz = z if zz is None else zz
        cc = c if cc is None else cc
        return (yy * NX + xx, zz * 2 + cc)

    def remote(src, dst, send, recv, device):
        return pltpu.make_async_remote_copy(
            src_ref=src, dst_ref=dst, send_sem=send, recv_sem=recv, device_id=device, device_id_type=MESH
        )

    barrier = pltpu.get_barrier_semaphore()

    def greet(i, carry):
        pl.semaphore_signal(barrier, inc=1, device_id=at(zz=(z + i) % nz), device_id_type=MESH)
        return carry

    lax.fori_loop(1, nz, greet, 0)
    for d in range(1, NX):
        pl.semaphore_signal(barrier, inc=1, device_id=at(xx=(x + d) % NX), device_id_type=MESH)
    for d in range(NY):
        if d > 0:
            pl.semaphore_signal(barrier, inc=1, device_id=at(yy=(y + d) % NY), device_id_type=MESH)
        pl.semaphore_signal(barrier, inc=1, device_id=at(yy=(y + d) % NY, cc=1 - c), device_id_type=MESH)

    chosen = lab_ref[...] == plc_ref[...]
    onehot = jnp.where(chosen, 1.0, 0.0).astype(F32)
    row = lax.broadcasted_iota(jnp.int32, (tokens, tokens), 0)
    col = lax.broadcasted_iota(jnp.int32, (tokens, tokens), 1)
    below = jnp.where(col < row, 1.0, 0.0).astype(BF16)
    earlier = dot(below, onehot.astype(BF16))
    first_slot = lax.broadcasted_iota(jnp.int32, onehot.shape, 1).astype(F32) * float(CAP)
    slot = jnp.sum(onehot * (earlier + first_slot), axis=1, keepdims=True).astype(jnp.int32)
    st = jnp.where(slot == lax.broadcasted_iota(jnp.int32, (tokens, slots), 1), 1.0, 0.0).astype(BF16)
    st_ref[...] = st

    def fill(kind, values):
        sent = dot(st_ref[...], values, ((0,), (0,))).astype(BF16)
        zsrc[kind] = sent.reshape(nz, NY * CAP, width)

    out_row = lax.broadcasted_iota(jnp.int32, (slots, slots), 0)
    in_row = lax.broadcasted_iota(jnp.int32, (slots, slots), 1)
    a_y, a_z, a_s = out_row // rows, (out_row // CAP) % nz, out_row % CAP
    swap = jnp.where(in_row == a_z * (NY * CAP) + a_y * CAP + a_s, 1.0, 0.0).astype(BF16)

    def z_copy(src, dst, k, d):
        zz = (z + d) % nz
        return remote(src.at[zz], dst.at[z], z_send.at[k, d], z_recv.at[k, d], at(zz=zz))

    def z_local(src, dst, k):
        return pltpu.make_async_copy(src.at[z], dst.at[z], z_recv.at[k, 0])

    def z_start(src, dst, k):
        def body(i, carry):
            half = (i + 1) // 2
            d = jnp.where(i % 2 == 1, nz // 2 - half, nz // 2 + half)
            z_copy(src, dst, k, d).start()
            return carry

        lax.fori_loop(0, nz - 1, body, 0)
        z_local(src, dst, k).start()

    def z_wait(src, dst, k):
        z_local(src, dst, k).wait()

        def body(d, carry):
            zz = (z + nz - d) % nz
            remote(src.at[zz], dst.at[zz], z_send.at[k, d], z_recv.at[k, d], at(zz=zz)).wait_recv()
            return carry

        lax.fori_loop(1, nz, body, 0)

    def z_sent(src, dst, k):
        def body(d, carry):
            z_copy(src, dst, k, d).wait_send()
            return carry

        lax.fori_loop(1, nz, body, 0)

    fill(0, tok_ref[...])
    pl.semaphore_wait(barrier, (nz - 1) + (NX - 1) + (NY - 1) + NY)
    z_start(zsrc.at[0], zbuf.at[0], 0)

    def w_pair(s, cc):
        yy = 2 * c + s
        pairs = (
            (wup_ref.at[s], wup.at[:, pl.ds(pl.multiple_of(y * group, group), group)]),
            (wdn_ref.at[s], wdn.at[pl.ds(pl.multiple_of(y * group, group), group)]),
        )
        here = jnp.logical_and(yy == y, cc == c)
        far = [
            remote(src, dst, w_send.at[s, cc, i], w_recv.at[y, i], at(yy=yy, cc=cc))
            for i, (src, dst) in enumerate(pairs)
        ]
        near = [pltpu.make_async_copy(src, dst, w_recv.at[y, i]) for i, (src, dst) in enumerate(pairs)]
        return here, near, far

    for s in range(2):
        for cc in range(2):
            here, near, far = w_pair(s, cc)

            @pl.when(here)
            def _():
                for copy in near:
                    copy.start()

            @pl.when(jnp.logical_not(here))
            def _():
                for copy in far:
                    copy.start()

    fill(1, cot_ref[...])
    z_start(zsrc.at[1], zbuf.at[1], 1)

    def y_copies(src, dst, k):
        return [
            remote(src.at[(y + d) % NY], dst.at[y], y_send.at[k, d], y_recv.at[k, d], at(yy=(y + d) % NY))
            for d in (2, 1, 3)
        ]

    def y_local(src, dst, k):
        return pltpu.make_async_copy(src.at[y], dst.at[y], y_recv.at[k, 0])

    def y_start(src, dst, k):
        for copy in y_copies(src, dst, k):
            copy.start()
        y_local(src, dst, k).start()

    def y_wait(src, dst, k):
        for d in (1, 3, 2):
            yy = (y + NY - d) % NY
            remote(src.at[yy], dst.at[yy], y_send.at[k, d], y_recv.at[k, d], at(yy=yy)).wait_recv()
        y_local(src, dst, k).wait()

    def y_sent(src, dst, k):
        for copy in y_copies(src, dst, k):
            copy.wait_send()

    right, left, across = (x + 1) % NX, (x + 3) % NX, (x + 2) % NX

    def to_y(k):
        z_wait(zsrc.at[k], zbuf.at[k], k)
        moved = dot(swap, zbuf[k].reshape(slots, width)).astype(BF16)
        ysrc[k] = moved.reshape(NY, rows, width)
        y_start(ysrc.at[k], xbuf.at[k, x], k)

    def x_copy(k, way, step, mine=True):
        half = NY // 2
        if step == 0:
            block = xbuf.at[k, x if mine else (left if way == 0 else right)]
        elif way == 0:
            block = xbuf.at[k, left if mine else across, 0:half]
        else:
            block = xbuf.at[k, right if mine else across, half:NY]
        return remote(
            block, block, x_send.at[k, way, step], x_recv.at[k, way, step], at(xx=right if way == 0 else left)
        )

    def to_x(k):
        y_wait(ysrc.at[k], xbuf.at[k, x], k)
        x_copy(k, 0, 0).start()
        x_copy(k, 1, 0).start()

    def pass_on(k):
        x_copy(k, 0, 0, False).wait_recv()
        x_copy(k, 0, 1).start()
        x_copy(k, 1, 0, False).wait_recv()
        x_copy(k, 1, 1).start()

    def last_x(k):
        x_copy(k, 0, 1, False).wait_recv()
        x_copy(k, 1, 1, False).wait_recv()

    half_width = wup.shape[1] // 2

    def forward(b):
        block = xbuf[0, b].reshape(chunk, width)
        pre = dot(block, wup[...])
        value, grad = gelu_parts(pre)
        slope[b] = grad
        hidden = value.astype(BF16)
        for h in range(2):
            hid[h, b] = hidden[:, h * half_width : (h + 1) * half_width]
        part[b] = dot(hidden, wdn[...]).astype(BF16)

    def backward(b):
        block = xbuf[1, b].reshape(chunk, width)
        back = dot(block, wdn[...], ((1,), (1,)))
        grad = (back * slope[b]).astype(BF16)
        for h in range(2):
            hg[h, b] = grad[:, h * half_width : (h + 1) * half_width]

    def rs_copy(d):
        xx = (x + d) % NX
        return remote(part.at[xx], rsbuf.at[d - 1], rs_send.at[d], rs_recv.at[d], at(xx=xx))

    to_y(0)
    to_x(0)
    for yy in range(NY):
        pltpu.make_async_copy(wup_ref.at[0], wup.at[:, yy * group : (yy + 1) * group], w_recv.at[yy, 0]).wait()
        pltpu.make_async_copy(wdn_ref.at[0], wdn.at[yy * group : (yy + 1) * group], w_recv.at[yy, 1]).wait()
    forward(x)
    pass_on(0)
    forward(right)
    rs_copy(1).start()
    forward(left)
    rs_copy(3).start()
    to_y(1)
    last_x(0)
    forward(across)
    rs_copy(2).start()
    to_x(1)
    backward(x)
    total = part[x].astype(F32)
    for d in (1, 3, 2):
        rs_copy(d).wait_recv()
        total = total + rsbuf[d - 1].astype(F32)
    ysend[...] = total.astype(BF16).reshape(NY, rows, width)
    y_start(ysend, yret, 2)
    pass_on(1)
    backward(right)
    backward(left)
    y_wait(ysend, yret, 2)
    back_row = lax.broadcasted_iota(jnp.int32, (slots, slots), 0)
    from_row = lax.broadcasted_iota(jnp.int32, (slots, slots), 1)
    b_z, b_y, b_s = back_row // (NY * CAP), (back_row // CAP) % NY, back_row % CAP
    unswap = jnp.where(from_row == b_y * rows + b_z * CAP + b_s, 1.0, 0.0).astype(BF16)
    moved = dot(unswap, yret[...].reshape(slots, width)).astype(BF16)
    zsend[...] = moved.reshape(nz, NY * CAP, width)
    z_start(zsend, zret, 2)
    last_x(1)
    backward(across)

    everything = NX * chunk
    flat_x = xbuf[0].reshape(everything, width)
    flat_c = xbuf[1].reshape(everything, width)

    def grads(h):
        up = dot(flat_x, hg[h].reshape(everything, half_width), ((0,), (0,)))
        down = dot(hid[h].reshape(everything, half_width), flat_c, ((0,), (0,)))
        return up, down

    up, down = grads(1 - c)
    gs_up[...] = up
    gs_dn[...] = down
    swap_up = remote(gs_up, gr_up, g_send.at[0], g_recv.at[0], at(cc=1 - c))
    swap_dn = remote(gs_dn, gr_dn, g_send.at[1], g_recv.at[1], at(cc=1 - c))
    swap_up.start()
    swap_dn.start()
    up, down = grads(c)
    swap_up.wait_recv()
    up = (up + gr_up[...]).astype(BF16)
    swap_dn.wait_recv()
    down = (down + gr_dn[...]).astype(BF16)
    owner, mine = y // 2, y % 2

    def gy_copies(k):
        yy = 2 * c + k
        gy_up[k] = up[:, k * group : (k + 1) * group]
        gy_dn[k] = down[k * group : (k + 1) * group]
        pairs = ((gy_up.at[k], gf_up.at[mine]), (gy_dn.at[k], gf_dn.at[mine]))
        far = [
            remote(src, dst, gy_send.at[k, i], gy_recv.at[mine, i], at(yy=yy, cc=owner))
            for i, (src, dst) in enumerate(pairs)
        ]
        near = [pltpu.make_async_copy(src, dst, gy_recv.at[mine, i]) for i, (src, dst) in enumerate(pairs)]
        return yy == y, near, far

    going = [gy_copies(k) for k in range(2)]
    for here, near, far in going:

        @pl.when(here)
        def _():
            for copy in near:
                copy.start()

        @pl.when(jnp.logical_not(here))
        def _():
            for copy in far:
                copy.start()

    z_wait(zsend, zret, 2)
    expert_out = dot(st_ref[...], zret[...].reshape(slots, width)).astype(BF16)
    field = tok_ref[...].astype(F32) + expert_out.astype(F32)
    logits = lax.dot_general(
        field, head_ref[...], (((1,), (0,)), ((), ())), precision=lax.Precision.HIGHEST, preferred_element_type=F32
    )
    positive = jnp.maximum(logits, 0.0) + jnp.log1p(jnp.exp(-jnp.abs(logits))) + 0.1
    mass = jnp.sum(jnp.where(row == col, mass_ref[...], 0.0), axis=1, keepdims=True)
    fine_ref[...] = mass * positive / jnp.sum(positive, axis=1, keepdims=True)

    for s in range(2):
        pltpu.make_async_copy(gy_up.at[0], gf_up.at[s], gy_recv.at[s, 0]).wait()
        upn_ref[s], umn_ref[s], usn_ref[s] = adam_step(wup_ref[s], um_ref[s], us_ref[s], gf_up[s].astype(F32))
        pltpu.make_async_copy(gy_dn.at[0], gf_dn.at[s], gy_recv.at[s, 1]).wait()
        dnn_ref[s], dmn_ref[s], dsn_ref[s] = adam_step(wdn_ref[s], dm_ref[s], ds_ref[s], gf_dn[s].astype(F32))

    for k in range(2):
        z_sent(zsrc.at[k], zbuf.at[k], k)
        y_sent(ysrc.at[k], xbuf.at[k, x], k)
        for way in range(2):
            for step in range(2):
                x_copy(k, way, step).wait_send()
    z_sent(zsend, zret, 2)
    y_sent(ysend, yret, 2)
    for d in range(1, NX):
        rs_copy(d).wait_send()
    swap_up.wait_send()
    swap_dn.wait_send()
    for s in range(2):
        for cc in range(2):
            here, near, far = w_pair(s, cc)

            @pl.when(jnp.logical_not(here))
            def _():
                for copy in far:
                    copy.wait_send()

    for here, near, far in going:

        @pl.when(jnp.logical_not(here))
        def _():
            for copy in far:
                copy.wait_send()


def local(
    tokens, cotangent, labels, placement, mass, w_head, w_up, w_down,
    up_moment, up_square, down_moment, down_square,
):
    nz = lax.axis_size("expert") // 2
    count, width = tokens.shape
    group = w_up.shape[2]
    full = NY * group
    slots = nz * NY * CAP
    rows = nz * CAP
    chunk = NY * rows
    vmem = pl.BlockSpec(memory_space=pltpu.VMEM)
    dma = pltpu.SemaphoreType.DMA
    shape = jax.ShapeDtypeStruct
    up_shape, down_shape = shape(w_up.shape, BF16), shape(w_down.shape, BF16)
    outs = pl.pallas_call(
        functools.partial(kernel, nz),
        out_shape=(
            shape((count, w_head.shape[1]), F32),
            up_shape, down_shape, up_shape, up_shape, down_shape, down_shape,
        ),
        in_specs=[vmem] * 12,
        out_specs=[vmem] * 7,
        scratch_shapes=[
            pltpu.VMEM((count, slots), BF16),
            pltpu.VMEM((2, nz, NY * CAP, width), BF16),
            pltpu.VMEM((2, nz, NY * CAP, width), BF16),
            pltpu.VMEM((2, NY, rows, width), BF16),
            pltpu.VMEM((2, NX, NY, rows, width), BF16),
            pltpu.VMEM((width, full), BF16),
            pltpu.VMEM((full, width), BF16),
            pltpu.VMEM((2, NX, chunk, full // 2), BF16),
            pltpu.VMEM((NX, chunk, full), F32),
            pltpu.VMEM((2, NX, chunk, full // 2), BF16),
            pltpu.VMEM((NX, chunk, width), BF16),
            pltpu.VMEM((NX - 1, chunk, width), BF16),
            pltpu.VMEM((NY, rows, width), BF16),
            pltpu.VMEM((NY, rows, width), BF16),
            pltpu.VMEM((nz, NY * CAP, width), BF16),
            pltpu.VMEM((nz, NY * CAP, width), BF16),
            pltpu.VMEM((width, full // 2), F32),
            pltpu.VMEM((full // 2, width), F32),
            pltpu.VMEM((width, full // 2), F32),
            pltpu.VMEM((full // 2, width), F32),
            pltpu.VMEM((2, width, group), BF16),
            pltpu.VMEM((2, group, width), BF16),
            pltpu.VMEM((2, width, group), BF16),
            pltpu.VMEM((2, group, width), BF16),
            dma((2, 2, 2)), dma((NY, 2)),
            dma((3, nz)), dma((3, nz)),
            dma((3, NY)), dma((3, NY)),
            dma((2, 2, 2)), dma((2, 2, 2)),
            dma((NX,)), dma((NX,)),
            dma((2,)), dma((2,)),
            dma((2, 2)), dma((2, 2)),
        ],
        compiler_params=pltpu.CompilerParams(
            collective_id=0, has_side_effects=True, vmem_limit_bytes=48 * 1024 * 1024
        ),
    )(
        tokens, cotangent, labels, placement[None, :], mass[None, :], w_head, w_up, w_down,
        up_moment, up_square, down_moment, down_square,
    )
    return tuple(outs)


def solution(mesh):
    by_token = P(("dp", "expert"), None)
    up, down = P("expert", None, "dp"), P("expert", "dp", None)
    return jax.shard_map(
        local,
        mesh=mesh,
        in_specs=(
            by_token, by_token, by_token, P(), P(("dp", "expert")), P(),
            up, down, up, up, down, down,
        ),
        out_specs=(by_token, up, down, up, up, down, down),
        check_vma=False,
    )
```

time: 304 us -> 96.8 us (0.32)
  waiting for transfers between devices: 169 us -> 0 us
  Pallas kernels: 0 us -> 82.4 us
  blocking collectives: 73.5 us -> 0 us
  matrix products: 18.9 us -> 0 us
  starting transfers between devices: 14.8 us -> 0 us
  between operations: 14 us -> 0.71 us
  local copies, waits for them, and re-layouts: 10 us -> 13.1 us
    all_gather x2 -> x0, waiting for transfers between devices: 114 us -> none  [the longest x1 58.6 us: local(): piece_x = lax.all_gather(recv_x, 'dp', axis=1, tiled=True)]
    pallas_call x0 -> x1, Pallas kernels: none -> 82.4 us  [local(): pl.pallas_call(functools.partial(kernel, nz), out_shape=(shape((count, w_...]
    all_to_all x2 -> x0, blocking collectives: 73.5 us -> none  [the longest x1 38.5 us: local(): lax.all_to_all(send_x, 'expert', split_axis=1, concat_axis=1, tiled=True)]
    reduce_scatter x1 -> x0, waiting for transfers between devices: 55.1 us -> none  [local(): lax.psum_scatter(jnp.einsum('rkf,kfd->rkd', hidden_all, w_down, preferred...]
    dot_general x5 -> x0, matrix products: 18.9 us -> none  [the longest x1 7.45 us: outer_in(): jnp.einsum('krd,krf->kdf', rows_x, hidden_grad, preferred_element_type=jn...]
    all_to_all x1 -> x0, starting transfers between devices: 14.6 us -> none  [local(): lax.all_to_all(outgoing, 'expert', split_axis=1, concat_axis=1, tiled=True)]
    unnamed x14 -> x28, local copies, waits for them, and re-layouts: 0.04 us -> 12.5 us
    reshape x9 -> x0, local copies, waits for them, and re-layouts: 3.75 us -> none  [the longest x2 1.83 us: local(): jnp.swapaxes(summed, 0, 1).reshape(local_count, holders, capacity, width)]
  transfers between devices with their start and end apart: 4 -> 0, of which waited for: 3 -> 0; matrix products, arithmetic and copies ran while one was open for 5% -> 0% of each run, Pallas kernels for 0% -> 0%
where the time goes in v1:
time: 96.8 us; the launch traced here: 96.2 us
  Pallas kernels  82.4 us (85%)
  local copies, waits for them, and re-layouts  13.1 us (14%)
    pallas_call x1, Pallas kernels, local(): pl.pallas_call(functools.partial(kernel, nz), out_shape=(shape((count, w_...  82.4 us
    unnamed x28, local copies, waits for them, and re-layouts  12.5 us

profile of v1, /device:TPU:1, one launch (start us, length us, event | category | flops | bytes accessed | tf_op | source)
XLA Modules:
  0.0 96.2 jit_solution(5399850190463706866)
XLA Ops:
  0.6 0.0 copy-start
  0.6 0.8 copy.19.lab_ref
  1.4 0.0 copy-start.8
  1.5 0.0 copy-start.9
  1.5 0.9 copy.20.head_ref
  2.4 0.0 copy-done
  2.4 0.0 copy-done.8
  2.4 0.0 copy-done.9
  2.4 0.0 copy-start.1
  2.4 0.9 copy-done.1
  3.3 0.0 copy-start.2
  3.3 0.9 copy-done.2
  4.3 0.0 copy-start.3
  4.3 0.9 copy-done.3
  5.2 0.0 copy-start.4
  5.3 0.9 copy-done.4
  6.2 0.0 copy-start.5
  6.2 0.9 copy-done.5
  7.1 0.0 copy-start.6
  7.2 0.9 copy-done.6
  8.1 0.0 copy-start.7
  8.1 0.9 copy-done.7
  9.0 82.4 %shard_map.171 = (f32[128,16]{1,0:T(8,128)S(1)}, bf16[2,512,128]{2,1,0:T(8,128)(2,1)S(1)}, bf16[2,128,512]{2,1,0:T(8,128)(2,1)S(1)}, bf16[2,512,128]{2,1,0:T(8,1...) custom-call(bf16[128,512]{1,0:T(8,128)(2,1)S(1)} %copy-done.6, ...), custom_call_target="tpu_custom_call" | custom-call | tf_op jit(solution)/shard_map/pallas_call | solution.py:406
  91.3 0.7 copy.21
  92.0 0.7 copy.28
  92.7 0.7 copy.29
  93.4 0.7 copy.30
  94.1 0.7 copy.31
  94.8 0.7 copy.32
  95.5 0.7 copy.33
Async XLA Ops:
  0.6 1.7 %copy-start = (bf16[2,512,128]{2,1,0:T(8,128)(2,1)S(1)}, bf16[2,512,128]{2,1,0:T(8,128)(2,1)}, u32[]{:S(2)}) copy-start(bf16[2,512,128]{2,1,0:T(8,128)(2,1)} %wup_ref.1) | copy-start | bytes 786436
  1.4 0.9 copy-start.8
  1.5 0.9 copy-start.9
  2.4 1.0 copy-start.1
  3.3 0.9 copy-start.2
  4.3 0.9 copy-start.3
  5.2 0.9 copy-start.4
  6.2 0.9 copy-start.5
  7.1 0.9 copy-start.6
  8.1 0.9 copy-start.7

commit v2 on v0

v2 whole, which is shorter than its diff:
```python
import jax
import jax.numpy as jnp
from jax import lax
from jax.experimental import pallas as pl
from jax.experimental.pallas import tpu as pltpu
from jax.sharding import PartitionSpec as P

MESH = pl.DeviceIdType.MESH
F32 = jnp.float32
BF16 = jnp.bfloat16

CAP = 4
NX = 4
NY = 4
NZ = 16
SET = NZ // 2

beta_first = 0.9
beta_second = 0.95
correct_first = 1.0 - 0.9**20
correct_second = 1.0 - 0.95**20
learn_rate = 0.002
adam_epsilon = 1e-08


def gelu_parts(pre):
    normal_cdf = 0.5 * (1.0 + lax.erf(pre * 0.7071067811865476))
    density = jnp.exp(-0.5 * pre * pre) * 0.3989422804014327
    return (pre * normal_cdf, normal_cdf + pre * density)


def adam_step(weight, first, second, grad):
    new_first = beta_first * first.astype(F32) + (1.0 - beta_first) * grad
    new_second = beta_second * second.astype(F32) + (1.0 - beta_second) * grad * grad
    update = new_first / correct_first / (jnp.sqrt(new_second / correct_second) + adam_epsilon)
    moved = weight.astype(F32) - learn_rate * update
    return moved.astype(BF16), new_first.astype(BF16), new_second.astype(BF16)


def dot(a, b, contract=((1,), (0,))):
    return lax.dot_general(a, b, (contract, ((), ())), preferred_element_type=F32)


def kernel(
    tok_hbm, cot_hbm, lab_hbm, plc_hbm, mass_hbm, head_hbm, wup_ref, wdn_ref,
    fine_ref, gf_up, gf_dn,
    tok_ref, cot_ref, lab_ref, plc_ref, mass_ref, head_ref,
    ent_ref, ext_ref, to_rows, to_msgs, zsrc, zbuf, xbuf, wup, wdn, hid, slope, hg, part, rsbuf, zsend, zret, gs_up, gs_dn, gr_up, gr_dn, gy_up, gy_dn,
    in_sem, w_send, w_recv, ws_send, ws_recv, z_send, z_recv, x_send, x_recv,
    rs_send, rs_recv, g_send, g_recv, gy_send, gy_recv,
):
    dp = lax.axis_index("dp")
    ex = lax.axis_index("expert")
    y, x = dp // NX, dp % NX
    z, c = ex // 2, ex % 2
    tokens, width = tok_ref.shape
    group = wup_ref.shape[2]
    slots = NZ * NY * CAP
    count = SET * NY
    chunk = count * CAP
    message = zsrc.shape[2]
    lanes = zsrc.shape[3]
    quarters = width // lanes
    right, left, across = (x + 1) % NX, (x + 3) % NX, (x + 2) % NX

    def at(yy=None, xx=None, zz=None, cc=None):
        yy = y if yy is None else yy
        xx = x if xx is None else xx
        zz = z if zz is None else zz
        cc = c if cc is None else cc
        return (yy * NX + xx, zz * 2 + cc)

    def up_z(d):
        return z + d - jnp.where(z + d >= NZ, NZ, 0)

    def down_z(d):
        return z - d + jnp.where(z < d, NZ, 0)

    y_up = [(y + e) % NY for e in range(NY)]
    y_down = [y_up[(NY - e) % NY] for e in range(NY)]

    def remote(src, dst, send, recv, device):
        return pltpu.make_async_remote_copy(
            src_ref=src, dst_ref=dst, send_sem=send, recv_sem=recv, device_id=device, device_id_type=MESH
        )

    barrier = pltpu.get_barrier_semaphore()

    def greet(i, carry):
        for e in range(NY):
            pl.semaphore_signal(barrier, inc=1, device_id=at(yy=y_up[e], zz=up_z(i)), device_id_type=MESH)
        return carry

    inbound = [
        pltpu.make_async_copy(src, dst, in_sem.at[i])
        for i, (src, dst) in enumerate(
            (
                (lab_hbm, lab_ref), (plc_hbm, plc_ref), (tok_hbm, tok_ref),
                (cot_hbm, cot_ref), (mass_hbm, mass_ref), (head_hbm, head_ref),
            )
        )
    ]
    lax.fori_loop(1, NZ, greet, 0)
    for copy in inbound:
        copy.start()
    for d in range(1, NX):
        pl.semaphore_signal(barrier, inc=1, device_id=at(xx=(x + d) % NX), device_id_type=MESH)
    for e in range(NY):
        if e > 0:
            pl.semaphore_signal(barrier, inc=1, device_id=at(yy=y_up[e]), device_id_type=MESH)
        pl.semaphore_signal(barrier, inc=1, device_id=at(yy=y_up[e], cc=1 - c), device_id_type=MESH)

    def iota(shape, dim):
        return lax.broadcasted_iota(jnp.int32, shape, dim)

    def upright(value):
        size = value.shape[1]
        return jnp.sum(jnp.where(iota((size, size), 0) == iota((size, size), 1), value, 0), axis=1, keepdims=True)

    def one_hot(a, b):
        return jnp.where(a == b, 1.0, 0.0).astype(BF16)

    inbound[0].wait()
    inbound[1].wait()
    chosen = jnp.where(upright(plc_ref[...]) == lab_ref[...], 1.0, 0.0).astype(F32)
    before = jnp.where(iota((tokens, tokens), 0) < iota((tokens, tokens), 1), 1.0, 0.0).astype(BF16)
    earlier = dot(chosen.astype(BF16), before)
    first_slot = (iota(chosen.shape, 0) * CAP).astype(F32)
    slot = jnp.sum(chosen * (earlier + first_slot), axis=0, keepdims=True).astype(jnp.int32)
    key = jnp.concatenate([slot * quarters + q for q in range(quarters)], axis=1)

    def message_key(shape, dim):
        r = iota(shape, dim)
        return ((r // message) * CAP + r % CAP) * quarters + (r // CAP) % quarters

    ent_ref[...] = one_hot(message_key((slots * quarters, 1), 0), key)

    def stacked(value):
        return jnp.concatenate([value[:, q * lanes : (q + 1) * lanes] for q in range(quarters)], axis=0)

    def spread(value):
        size = value.shape[0] // quarters
        return jnp.concatenate([value[q * size : (q + 1) * size] for q in range(quarters)], axis=1)

    def fill(k, values):
        sent = dot(ent_ref[...], stacked(values)).astype(BF16)
        zsrc[k] = sent.reshape(NZ * NY, message, lanes)

    def prepare():
        size = chunk * quarters

        def place(shape, dim):
            r = iota(shape, dim)
            return ((r % chunk) // CAP) * message + (r // chunk) * CAP + r % CAP

        to_rows[...] = one_hot(place((size, 1), 0), iota((1, size), 1))
        to_msgs[...] = one_hot(iota((size, 1), 0), place((1, size), 1))
        columns = upright(slot)
        upright_key = jnp.concatenate([columns * quarters + q for q in range(quarters)], axis=0)
        ext_ref[...] = one_hot(upright_key, message_key((1, slots * quarters), 1))

    far_first, near_first = NZ // 2 - SET // 2 + 1, NZ - SET // 2 + 1
    self_index = NZ - near_first

    def z_loop(s, step, own):
        def all_y(d, j):
            for e in (2, 1, 3, 0):
                step(d, e, j * NY + e)

        def body(i, carry):
            if s == 0:
                all_y(far_first + i, i)
                all_y(far_first + SET - 1 - i, SET - 1 - i)
            else:
                all_y(near_first + i, i)
                all_y(self_index - i, 2 * self_index - i)
            return carry

        if s == 0:
            lax.fori_loop(0, SET // 2, body, 0)
        else:
            all_y(SET // 2, SET - 1)
            lax.fori_loop(0, self_index, body, 0)
            for e in (2, 1, 3):
                step(0, e, self_index * NY + e)
            own()

    def z_start(k, s):
        def step(d, e, i):
            zz, yy = up_z(d), y_up[e]
            remote(
                zsrc.at[k, zz * NY + yy], zbuf.at[k, s, i], z_send.at[k, s], z_recv.at[k, s], at(yy=yy, zz=zz)
            ).start()

        def local():
            pltpu.make_async_copy(
                zsrc.at[k, z * NY + y], zbuf.at[k, 1, self_index * NY], z_recv.at[k, 1]
            ).start()

        z_loop(s, step, local)

    def zr_start(s):
        def step(d, e, i):
            zz, yy = down_z(d), y_down[e]
            remote(
                zsend.at[s, i], zret.at[z * NY + y], z_send.at[2, s], z_recv.at[2, 0], at(yy=yy, zz=zz)
            ).start()

        def local():
            pltpu.make_async_copy(
                zsend.at[1, self_index * NY], zret.at[z * NY + y], z_recv.at[2, 0]
            ).start()

        z_loop(s, step, local)

    def z_wait(k, s):
        pltpu.make_async_copy(zbuf.at[k, s], zbuf.at[k, s], z_recv.at[k, s]).wait()

    def zr_wait():
        pltpu.make_async_copy(zret, zret, z_recv.at[2, 0]).wait()

    def z_sent(k, s):
        out = zsrc.at[0, 0 : count - s]
        pltpu.make_async_copy(out, out, z_send.at[k, s]).wait()

    inbound[2].wait()
    fill(0, tok_ref[...])
    pl.semaphore_wait(barrier, (NZ * NY - 1) + (NX - 1) + NY)
    z_start(0, 0)
    z_start(0, 1)

    def w_pair(s, i):
        yy = 2 * c + s
        piece = pl.ds(pl.multiple_of(y * group, group), group)
        src, dst = ((wup_ref.at[s], wup.at[:, piece]), (wdn_ref.at[s], wdn.at[piece]))[i]
        here = jnp.logical_and(yy == y, c == i)

        def far():
            return remote(src, dst, w_send.at[s, i], w_recv.at[y], at(yy=yy, cc=i))

        def near():
            return pltpu.make_async_copy(src, dst, w_recv.at[y])

        return here, near, far

    def w_start():
        for s in range(2):
            for i in range(2):
                here, near, far = w_pair(s, i)

                @pl.when(here)
                def _():
                    near().start()

                @pl.when(jnp.logical_not(here))
                def _():
                    far().start()

    def w_sent():
        for s in range(2):
            for i in range(2):
                here, near, far = w_pair(s, i)

                @pl.when(jnp.logical_not(here))
                def _():
                    far().wait_send()

    def w_share(i):
        ref = (wup, wdn)[i]
        return remote(ref, ref, ws_send.at[0], ws_recv.at[0], at(cc=1 - c))

    def w_pass():
        @pl.when(c == 0)
        def _():
            for yy in range(NY):
                pltpu.make_async_copy(wup_ref.at[0], wup.at[:, yy * group : (yy + 1) * group], w_recv.at[yy]).wait()
            w_share(0).start()

        @pl.when(c == 1)
        def _():
            for yy in range(NY):
                pltpu.make_async_copy(wdn_ref.at[0], wdn.at[yy * group : (yy + 1) * group], w_recv.at[yy]).wait()
            w_share(1).start()

    def w_done():
        @pl.when(c == 0)
        def _():
            w_share(1).wait_recv()
            w_share(0).wait_send()

        @pl.when(c == 1)
        def _():
            w_share(0).wait_recv()
            w_share(1).wait_send()

    w_start()
    inbound[3].wait()
    fill(1, cot_ref[...])

    middle = chunk // 2
    halves = (pl.ds(0, middle), pl.ds(middle, middle))

    def x_copy(k, s, way, step, mine=True):
        if step == 0:
            block = xbuf.at[k, s, x if mine else (left if way == 0 else right)]
        elif way == 0:
            block = xbuf.at[k, s, left if mine else across, halves[0]]
        else:
            block = xbuf.at[k, s, right if mine else across, halves[1]]
        return remote(
            block, block, x_send.at[k, s, way, step], x_recv.at[k, s, way, step],
            at(xx=right if way == 0 else left),
        )

    def to_x(k, s):
        z_wait(k, s)
        moved = dot(to_rows[...], zbuf[k, s].reshape(chunk * quarters, lanes)).astype(BF16)
        xbuf[k, s, x] = spread(moved)
        x_copy(k, s, 0, 0).start()
        x_copy(k, s, 1, 0).start()

    def pass_on(k, s):
        for way in range(2):
            x_copy(k, s, way, 0, False).wait_recv()
            x_copy(k, s, way, 1).start()

    def last_x(k, s):
        for way in range(2):
            x_copy(k, s, way, 1, False).wait_recv()

    def x_sent(k, s):
        for way in range(2):
            for step in range(2):
                x_copy(k, s, way, step).wait_send()

    half_width = wup.shape[1] // 2

    def forward(s, b):
        block = xbuf[0, s, b]
        value, grad = gelu_parts(dot(block, wup[...]))
        slope[s, b] = grad
        hidden = value.astype(BF16)
        for h in range(2):
            hid[h, s, b] = hidden[:, h * half_width : (h + 1) * half_width]
        part[s, b] = dot(hidden, wdn[...]).astype(BF16)

    def backward(s, b):
        block = xbuf[1, s, b]
        grad = (dot(block, wdn[...], ((1,), (1,))) * slope[s, b]).astype(BF16)
        for h in range(2):
            hg[h, s, b] = grad[:, h * half_width : (h + 1) * half_width]

    def rs_copy(s, d):
        xx = (x + d) % NX
        return remote(part.at[s, xx], rsbuf.at[s, d - 1], rs_send.at[s, d], rs_recv.at[s, d], at(xx=xx))

    def rs_sent(s):
        for d in range(1, NX):
            rs_copy(s, d).wait_send()

    def return_z(s):
        total = part[s, x].astype(F32)
        for d in (1, 3, 2):
            rs_copy(s, d).wait_recv()
            total = total + rsbuf[s, d - 1].astype(F32)
        moved = dot(to_msgs[...], stacked(total.astype(BF16))).astype(BF16)
        zsend[s] = moved.reshape(count, message, lanes)
        zr_start(s)

    everything = 2 * NX * chunk

    def grad_up(h):
        return dot(xbuf[0].reshape(everything, width), hg[h].reshape(everything, half_width), ((0,), (0,)))

    def grad_down(h):
        return dot(hid[h].reshape(everything, half_width), xbuf[1].reshape(everything, width), ((0,), (0,)))

    swap_up = remote(gs_up, gr_up, g_send.at[0], g_recv.at[0], at(cc=1 - c))
    swap_dn = remote(gs_dn, gr_dn, g_send.at[1], g_recv.at[1], at(cc=1 - c))
    owner, mine = y // 2, y % 2

    def gy_pair(k, i):
        yy = 2 * c + k
        src, dst = ((gy_up.at[k], gf_up.at[mine]), (gy_dn.at[k], gf_dn.at[mine]))[i]

        def far():
            return remote(src, dst, gy_send.at[k, i], gy_recv.at[mine, i], at(yy=yy, cc=owner))

        def near():
            return pltpu.make_async_copy(src, dst, gy_recv.at[mine, i])

        return yy == y, near, far

    def gy_start(i):
        for k in range(2):
            here, near, far = gy_pair(k, i)

            @pl.when(here)
            def _():
                near().start()

            @pl.when(jnp.logical_not(here))
            def _():
                far().start()

    def gy_sent(i):
        for k in range(2):
            here, near, far = gy_pair(k, i)

            @pl.when(jnp.logical_not(here))
            def _():
                far().wait_send()

    def gy_wait(i):
        src, dst = ((gy_up, gf_up), (gy_dn, gf_dn))[i]
        for s in range(2):
            pltpu.make_async_copy(src.at[0], dst.at[s], gy_recv.at[s, i]).wait()

    def head():
        zr_wait()
        expert_out = spread(dot(ext_ref[...], zret[...].reshape(slots * quarters, lanes)).astype(BF16))
        field = tok_ref[...].astype(F32) + expert_out.astype(F32)
        inbound[4].wait()
        inbound[5].wait()
        logits = lax.dot_general(
            head_ref[...], field, (((1,), (1,)), ((), ())), precision=lax.Precision.HIGHEST, preferred_element_type=F32
        )
        positive = jnp.maximum(logits, 0.0) + jnp.log1p(jnp.exp(-jnp.abs(logits))) + 0.1
        fine_ref[...] = mass_ref[...] * positive / jnp.sum(positive, axis=0, keepdims=True)

    def forward_near(s):
        forward(s, right)
        rs_copy(s, 1).start()
        forward(s, left)
        rs_copy(s, 3).start()

    def forward_far(s):
        forward(s, across)
        rs_copy(s, 2).start()

    prepare()
    to_x(0, 0)
    z_sent(0, 0)
    z_start(1, 0)
    w_pass()
    to_x(0, 1)
    z_sent(0, 1)
    z_start(1, 1)
    w_done()
    forward(0, x)
    pass_on(0, 0)
    forward(1, x)
    forward_near(0)
    pass_on(0, 1)
    last_x(0, 0)
    forward_far(0)
    forward_near(1)
    last_x(0, 1)
    forward_far(1)
    to_x(1, 0)
    return_z(0)
    backward(0, x)
    to_x(1, 1)
    pass_on(1, 0)
    return_z(1)
    backward(1, x)
    backward(0, right)
    backward(0, left)
    pass_on(1, 1)
    last_x(1, 0)
    backward(0, across)
    backward(1, right)
    backward(1, left)
    last_x(1, 1)
    gs_dn[...] = grad_down(1 - c)
    swap_dn.start()
    backward(1, across)
    gs_up[...] = grad_up(1 - c)
    swap_up.start()
    down = grad_down(c)
    swap_dn.wait_recv()
    down = (down + gr_dn[...]).astype(BF16)
    for k in range(2):
        gy_dn[k] = down[k * group : (k + 1) * group]
    gy_start(1)
    up = grad_up(c)
    swap_up.wait_recv()
    up = (up + gr_up[...]).astype(BF16)
    for k in range(2):
        gy_up[k] = up[:, k * group : (k + 1) * group]
    gy_start(0)
    head()
    gy_wait(1)
    gy_wait(0)

    for s in range(2):
        z_sent(1, s)
        z_sent(2, s)
        for k in range(2):
            x_sent(k, s)
        rs_sent(s)
    swap_up.wait_send()
    swap_dn.wait_send()
    gy_sent(0)
    gy_sent(1)
    w_sent()


def local(
    tokens, cotangent, labels, placement, mass, w_head, w_up, w_down,
    up_moment, up_square, down_moment, down_square,
):
    count, width = tokens.shape
    group = w_up.shape[2]
    full = NY * group
    slots = NZ * NY * CAP
    messages = SET * NY
    chunk = messages * CAP
    lanes = 128
    quarters = width // lanes
    message = quarters * CAP
    vmem = pl.BlockSpec(memory_space=pltpu.VMEM)
    hbm = pl.BlockSpec(memory_space=pl.ANY)
    dma = pltpu.SemaphoreType.DMA
    shape = jax.ShapeDtypeStruct
    pixels, experts = w_head.shape[1], placement.shape[0]
    fine, grad_up, grad_down = pl.pallas_call(
        kernel,
        out_shape=(shape((pixels, count), F32), shape(w_up.shape, BF16), shape(w_down.shape, BF16)),
        in_specs=[hbm] * 8,
        out_specs=[vmem] * 3,
        scratch_shapes=[
            pltpu.VMEM((count, width), BF16),
            pltpu.VMEM((count, width), BF16),
            pltpu.VMEM((1, count), jnp.int32),
            pltpu.VMEM((1, experts), jnp.int32),
            pltpu.VMEM((1, count), F32),
            pltpu.VMEM((pixels, width), F32),
            pltpu.VMEM((slots * quarters, count * quarters), BF16),
            pltpu.VMEM((count * quarters, slots * quarters), BF16),
            pltpu.VMEM((chunk * quarters, chunk * quarters), BF16),
            pltpu.VMEM((chunk * quarters, chunk * quarters), BF16),
            pltpu.VMEM((2, NZ * NY, message, lanes), BF16),
            pltpu.VMEM((2, 2, messages, message, lanes), BF16),
            pltpu.VMEM((2, 2, NX, chunk, width), BF16),
            pltpu.VMEM((width, full), BF16),
            pltpu.VMEM((full, width), BF16),
            pltpu.VMEM((2, 2, NX, chunk, full // 2), BF16),
            pltpu.VMEM((2, NX, chunk, full), F32),
            pltpu.VMEM((2, 2, NX, chunk, full // 2), BF16),
            pltpu.VMEM((2, NX, chunk, width), BF16),
            pltpu.VMEM((2, NX - 1, chunk, width), BF16),
            pltpu.VMEM((2, messages, message, lanes), BF16),
            pltpu.VMEM((NZ * NY, message, lanes), BF16),
            pltpu.VMEM((width, full // 2), F32),
            pltpu.VMEM((full // 2, width), F32),
            pltpu.VMEM((width, full // 2), F32),
            pltpu.VMEM((full // 2, width), F32),
            pltpu.VMEM((2, width, group), BF16),
            pltpu.VMEM((2, group, width), BF16),
            dma((6,)),
            dma((2, 2)), dma((NY,)),
            dma((1,)), dma((1,)),
            dma((3, 2)), dma((3, 2)),
            dma((2, 2, 2, 2)), dma((2, 2, 2, 2)),
            dma((2, NX)), dma((2, NX)),
            dma((2,)), dma((2,)),
            dma((2, 2)), dma((2, 2)),
        ],
        compiler_params=pltpu.CompilerParams(
            collective_id=0, has_side_effects=True, vmem_limit_bytes=56 * 1024 * 1024
        ),
    )(tokens, cotangent, labels.reshape(1, count), placement[None, :], mass[None, :], jnp.transpose(w_head), w_up, w_down)
    up = adam_step(w_up, up_moment, up_square, grad_up.astype(F32))
    down = adam_step(w_down, down_moment, down_square, grad_down.astype(F32))
    return jnp.transpose(fine), up[0], down[0], up[1], up[2], down[1], down[2]


def solution(mesh):
    by_token = P(("dp", "expert"), None)
    up, down = P("expert", None, "dp"), P("expert", "dp", None)
    return jax.shard_map(
        local,
        mesh=mesh,
        in_specs=(
            by_token, by_token, by_token, P(), P(("dp", "expert")), P(),
            up, down, up, up, down, down,
        ),
        out_specs=(by_token, up, down, up, up, down, down),
        check_vma=False,
    )
```

time: 304 us -> 82.4 us (0.27)
  waiting for transfers between devices: 169 us -> 0 us
  Pallas kernels: 0 us -> 77 us
  blocking collectives: 73.5 us -> 0 us
  matrix products: 18.9 us -> 0 us
  starting transfers between devices: 14.8 us -> 0 us
  between operations: 14 us -> 0.74 us
  local copies, waits for them, and re-layouts: 10 us -> 0.64 us
    all_gather x2 -> x0, waiting for transfers between devices: 114 us -> none  [the longest x1 58.6 us: local(): piece_x = lax.all_gather(recv_x, 'dp', axis=1, tiled=True)]
    pallas_call x0 -> x1, Pallas kernels: none -> 77 us  [local(): pl.pallas_call(kernel, out_shape=(shape((pixels, count), F32), shape(w_up...]
    all_to_all x2 -> x0, blocking collectives: 73.5 us -> none  [the longest x1 38.5 us: local(): lax.all_to_all(send_x, 'expert', split_axis=1, concat_axis=1, tiled=True)]
    reduce_scatter x1 -> x0, waiting for transfers between devices: 55.1 us -> none  [local(): lax.psum_scatter(jnp.einsum('rkf,kfd->rkd', hidden_all, w_down, preferred...]
    dot_general x5 -> x0, matrix products: 18.9 us -> none  [the longest x1 7.45 us: outer_in(): jnp.einsum('krd,krf->kdf', rows_x, hidden_grad, preferred_element_type=jn...]
    all_to_all x1 -> x0, starting transfers between devices: 14.6 us -> none  [local(): lax.all_to_all(outgoing, 'expert', split_axis=1, concat_axis=1, tiled=True)]
    convert_element_type x1 -> x2, other arithmetic: 0.09 us -> 3.94 us  [adam_step(): return (moved.astype(BF16), new_first.astype(BF16), new_second.astype(BF16))]
    reshape x9 -> x0, local copies, waits for them, and re-layouts: 3.75 us -> none  [the longest x2 1.83 us: local(): jnp.swapaxes(summed, 0, 1).reshape(local_count, holders, capacity, width)]
  transfers between devices with their start and end apart: 4 -> 0, of which waited for: 3 -> 0; matrix products, arithmetic and copies ran while one was open for 5% -> 0% of each run, Pallas kernels for 0% -> 0%
where the time goes in v2:
time: 82.4 us; the launch traced here: 82.3 us
  Pallas kernels  77 us (93%)
  other arithmetic  3.94 us (5%)
    pallas_call x1, Pallas kernels, local(): pl.pallas_call(kernel, out_shape=(shape((pixels, count), F32), shape(w_up...  77 us
    convert_element_type x2, other arithmetic, adam_step(): return (moved.astype(BF16), new_first.astype(BF16), new_second.astype(BF16))  3.94 us

profile of v2, /device:TPU:1, one launch (start us, length us, event | category | flops | bytes accessed | tf_op | source)
XLA Modules:
  0.0 82.3 jit_solution(10484732001028326998)
XLA Ops:
  0.6 0.0 copy-start
  0.6 0.0 copy-start.2
  0.7 0.0 copy-start.3
  0.7 77.0 %shard_map.171 = (f32[16,128]{1,0:T(8,128)}, bf16[2,512,128]{2,1,0:T(8,128)(2,1)}, bf16[2,128,512]{2,1,0:T(8,128)(2,1)}) custom-call(bf16[128,512]{1,0:T(8,128)(2,1)} %tok_hbm.1, bf16[128,512]{1,0:T(8,128)(2,1)} %cot_hbm.1, s32[1,128]{1,0:T(1,128)} %bitcast.7, s32[1,64]{1,0:T(1,128)} %bitcast.8, f32[1,128]{1,0:T(1,128)} %bitcast.9, f32[16,512]{1,0:T(8,128)} %bitcast.5, ...), custom_call_target="tpu_custom_call" | custom-call | tf_op jit(solution)/shard_map/pallas_call | solution.py:527
  77.6 0.0 copy-done
  77.7 0.0 copy-done.2
  77.7 0.0 copy-done.3
  77.7 0.0 copy-start.1
  77.7 0.0 copy-start.4
  77.7 0.0 copy-start.5
  77.7 0.0 copy-start.6
  77.7 2.5 %fusion.7 = (bf16[2,512,128]{2,1,0:T(8,128)(2,1)}, bf16[2,512,128]{2,1,0:T(8,128)(2,1)}, bf16[2,512,128]{2,1,0:T(8,128)(2,1)}) fusion(bf16[2,512,128]{2,1,0:T(8,128)(2,1)} %get-tuple-element.11, bf16[2,512,128]{2,1,0:T(8,128)(2,1)S(1)} %copy-done.2, bf16[2,512,128]{2,1,0:T(8,128)(2,1)S(1)} %copy-done.3, bf16[2,512,128]{2,1,0:T(8,128)(2,1)S(1)} %copy-done), kind=kLoop, calls=%fused_computation.13 | loop fusion | flops 2621440 | bytes 1835008 | tf_op jit(solution)/shard_map/convert_element_type | solution.py:37
  80.2 0.0 copy-done.1
  80.2 0.0 copy-done.4
  80.2 0.0 copy-done.5
  80.2 0.0 copy-done.6
  80.2 0.0 copy-start.7
  80.2 1.5 %fusion.6 = (bf16[2,128,512]{2,1,0:T(8,128)(2,1)}, bf16[2,128,512]{2,1,0:T(8,128)(2,1)}, bf16[2,128,512]{2,1,0:T(8,128)(2,1)}) fusion(bf16[2,128,512]{2,1,0:T(8,128)(2,1)S(1)} %copy-done.6, bf16[2,128,512]{2,1,0:T(8,128)(2,1)S(1)} %copy-done.4, bf16[2,128,512]{2,1,0:T(8,128)(2,1)S(1)} %copy-done.5, bf16[2,128,512]{2,1,0:T(8,128)(2,1)S(1)} %copy-done.1), kind=kLoop, calls=%fused_computation.12 | loop fusion | flops 2621440 | bytes 1835008 | tf_op jit(solution)/shard_map/convert_element_type | solution.py:37
  81.7 0.0 copy-done.7
  81.7 0.6 copy.20
Async XLA Ops:
  0.6 77.0 %copy-start = (bf16[2,512,128]{2,1,0:T(8,128)(2,1)S(1)}, bf16[2,512,128]{2,1,0:T(8,128)(2,1)}, u32[]{:S(2)}) copy-start(bf16[2,512,128]{2,1,0:T(8,128)(2,1)} %wup_ref.1) | copy-start | bytes 786436
  0.6 77.0 %copy-start.2 = (bf16[2,512,128]{2,1,0:T(8,128)(2,1)S(1)}, bf16[2,512,128]{2,1,0:T(8,128)(2,1)}, u32[]{:S(2)}) copy-start(bf16[2,512,128]{2,1,0:T(8,128)(2,1)} %param.21) | copy-start | bytes 786436
  0.7 77.0 %copy-start.3 = (bf16[2,512,128]{2,1,0:T(8,128)(2,1)S(1)}, bf16[2,512,128]{2,1,0:T(8,128)(2,1)}, u32[]{:S(2)}) copy-start(bf16[2,512,128]{2,1,0:T(8,128)(2,1)} %param.20) | copy-start | bytes 786436
  77.7 2.5 %copy-start.1 = (bf16[2,128,512]{2,1,0:T(8,128)(2,1)S(1)}, bf16[2,128,512]{2,1,0:T(8,128)(2,1)}, u32[]{:S(2)}) copy-start(bf16[2,128,512]{2,1,0:T(8,128)(2,1)} %wdn_ref.1) | copy-start | bytes 786436
  77.7 2.5 %copy-start.4 = (bf16[2,128,512]{2,1,0:T(8,128)(2,1)S(1)}, bf16[2,128,512]{2,1,0:T(8,128)(2,1)}, u32[]{:S(2)}) copy-start(bf16[2,128,512]{2,1,0:T(8,128)(2,1)} %param.23) | copy-start | bytes 786436
  77.7 2.5 %copy-start.5 = (bf16[2,128,512]{2,1,0:T(8,128)(2,1)S(1)}, bf16[2,128,512]{2,1,0:T(8,128)(2,1)}, u32[]{:S(2)}) copy-start(bf16[2,128,512]{2,1,0:T(8,128)(2,1)} %param.22) | copy-start | bytes 786436
  77.7 2.5 %copy-start.6 = (bf16[2,128,512]{2,1,0:T(8,128)(2,1)S(1)}, bf16[2,128,512]{2,1,0:T(8,128)(2,1)}, u32[]{:S(2)}) copy-start(bf16[2,128,512]{2,1,0:T(8,128)(2,1)} %get-tuple-element.12) | copy-start | bytes 786436
  80.2 1.5 %copy-start.7 = (f32[16,128]{1,0:T(8,128)S(1)}, f32[16,128]{1,0:T(8,128)}, u32[]{:S(2)}) copy-start(f32[16,128]{1,0:T(8,128)} %get-tuple-element.10) | copy-start | bytes 24580

commit v3 on v2

--- a/solution.py
+++ b/solution.py
@@ -226,8 +226,8 @@
     inbound[2].wait()
     fill(0, tok_ref[...])
     pl.semaphore_wait(barrier, (NZ * NY - 1) + (NX - 1) + NY)
+    z_start(0, 1)
     z_start(0, 0)
-    z_start(0, 1)
 
     def w_pair(s, i):
         yy = 2 * c + s
@@ -439,42 +439,42 @@
         rs_copy(s, 2).start()
 
     prepare()
+    to_x(0, 1)
+    w_pass()
+    pass_on(0, 1)
+    w_done()
+    forward(1, x)
+    z_sent(0, 1)
+    z_sent(0, 0)
+    z_start(1, 1)
+    z_start(1, 0)
+    forward_near(1)
     to_x(0, 0)
-    z_sent(0, 0)
-    z_start(1, 0)
-    w_pass()
-    to_x(0, 1)
-    z_sent(0, 1)
-    z_start(1, 1)
-    w_done()
+    last_x(0, 1)
+    forward_far(1)
     forward(0, x)
     pass_on(0, 0)
-    forward(1, x)
     forward_near(0)
-    pass_on(0, 1)
+    to_x(1, 1)
+    return_z(1)
     last_x(0, 0)
     forward_far(0)
-    forward_near(1)
-    last_x(0, 1)
-    forward_far(1)
+    backward(1, x)
+    pass_on(1, 1)
     to_x(1, 0)
+    backward(1, right)
+    backward(1, left)
     return_z(0)
+    last_x(1, 1)
+    backward(1, across)
     backward(0, x)
-    to_x(1, 1)
     pass_on(1, 0)
-    return_z(1)
-    backward(1, x)
     backward(0, right)
     backward(0, left)
-    pass_on(1, 1)
     last_x(1, 0)
-    backward(0, across)
-    backward(1, right)
-    backward(1, left)
-    last_x(1, 1)
     gs_dn[...] = grad_down(1 - c)
     swap_dn.start()
-    backward(1, across)
+    backward(0, across)
     gs_up[...] = grad_up(1 - c)
     swap_up.start()
     down = grad_down(c)

time: 82.4 us -> 79.6 us (0.966)
  Pallas kernels: 77 us -> 74.2 us
    pallas_call x1, Pallas kernels: 77 us -> 74.2 us  [local(): pl.pallas_call(kernel, out_shape=(shape((pixels, count), F32), shape(w_up...]
where the time goes in v3:
time: 79.6 us; the launch traced here: 79.5 us
  Pallas kernels  74.2 us (93%)
  other arithmetic  3.94 us (5%)
    pallas_call x1, Pallas kernels, local(): pl.pallas_call(kernel, out_shape=(shape((pixels, count), F32), shape(w_up...  74.2 us
    convert_element_type x2, other arithmetic, adam_step(): return (moved.astype(BF16), new_first.astype(BF16), new_second.astype(BF16))  3.94 us

profile of v3, /device:TPU:1, one launch (start us, length us, event | category | flops | bytes accessed | tf_op | source)
XLA Modules:
  0.0 79.5 jit_solution(10584964727164848263)
XLA Ops:
  0.6 0.0 copy-start
  0.6 0.0 copy-start.2
  0.7 0.0 copy-start.3
  0.7 74.2 %shard_map.171 = (f32[16,128]{1,0:T(8,128)}, bf16[2,512,128]{2,1,0:T(8,128)(2,1)}, bf16[2,128,512]{2,1,0:T(8,128)(2,1)}) custom-call(bf16[128,512]{1,0:T(8,128)(2,1)} %tok_hbm.1, bf16[128,512]{1,0:T(8,128)(2,1)} %cot_hbm.1, s32[1,128]{1,0:T(1,128)} %bitcast.7, s32[1,64]{1,0:T(1,128)} %bitcast.8, f32[1,128]{1,0:T(1,128)} %bitcast.9, f32[16,512]{1,0:T(8,128)} %bitcast.5, ...), custom_call_target="tpu_custom_call" | custom-call | tf_op jit(solution)/shard_map/pallas_call | solution.py:527
  74.8 0.0 copy-done
  74.9 0.0 copy-done.2
  74.9 0.0 copy-done.3
  74.9 0.0 copy-start.1
  74.9 0.0 copy-start.4
  74.9 0.0 copy-start.5
  74.9 0.0 copy-start.6
  74.9 2.5 %fusion.7 = (bf16[2,512,128]{2,1,0:T(8,128)(2,1)}, bf16[2,512,128]{2,1,0:T(8,128)(2,1)}, bf16[2,512,128]{2,1,0:T(8,128)(2,1)}) fusion(bf16[2,512,128]{2,1,0:T(8,128)(2,1)} %get-tuple-element.11, bf16[2,512,128]{2,1,0:T(8,128)(2,1)S(1)} %copy-done.2, bf16[2,512,128]{2,1,0:T(8,128)(2,1)S(1)} %copy-done.3, bf16[2,512,128]{2,1,0:T(8,128)(2,1)S(1)} %copy-done), kind=kLoop, calls=%fused_computation.13 | loop fusion | flops 2621440 | bytes 1835008 | tf_op jit(solution)/shard_map/convert_element_type | solution.py:37
  77.4 0.0 copy-done.1
  77.4 0.0 copy-done.4
  77.4 0.0 copy-done.5
  77.4 0.0 copy-done.6
  77.4 0.0 copy-start.7
  77.4 1.5 %fusion.6 = (bf16[2,128,512]{2,1,0:T(8,128)(2,1)}, bf16[2,128,512]{2,1,0:T(8,128)(2,1)}, bf16[2,128,512]{2,1,0:T(8,128)(2,1)}) fusion(bf16[2,128,512]{2,1,0:T(8,128)(2,1)S(1)} %copy-done.6, bf16[2,128,512]{2,1,0:T(8,128)(2,1)S(1)} %copy-done.4, bf16[2,128,512]{2,1,0:T(8,128)(2,1)S(1)} %copy-done.5, bf16[2,128,512]{2,1,0:T(8,128)(2,1)S(1)} %copy-done.1), kind=kLoop, calls=%fused_computation.12 | loop fusion | flops 2621440 | bytes 1835008 | tf_op jit(solution)/shard_map/convert_element_type | solution.py:37
  78.9 0.0 copy-done.7
  78.9 0.6 copy.20
Async XLA Ops:
  0.6 74.2 %copy-start = (bf16[2,512,128]{2,1,0:T(8,128)(2,1)S(1)}, bf16[2,512,128]{2,1,0:T(8,128)(2,1)}, u32[]{:S(2)}) copy-start(bf16[2,512,128]{2,1,0:T(8,128)(2,1)} %wup_ref.1) | copy-start | bytes 786436
  0.6 74.2 %copy-start.2 = (bf16[2,512,128]{2,1,0:T(8,128)(2,1)S(1)}, bf16[2,512,128]{2,1,0:T(8,128)(2,1)}, u32[]{:S(2)}) copy-start(bf16[2,512,128]{2,1,0:T(8,128)(2,1)} %param.21) | copy-start | bytes 786436
  0.7 74.2 %copy-start.3 = (bf16[2,512,128]{2,1,0:T(8,128)(2,1)S(1)}, bf16[2,512,128]{2,1,0:T(8,128)(2,1)}, u32[]{:S(2)}) copy-start(bf16[2,512,128]{2,1,0:T(8,128)(2,1)} %param.20) | copy-start | bytes 786436
  74.9 2.5 %copy-start.1 = (bf16[2,128,512]{2,1,0:T(8,128)(2,1)S(1)}, bf16[2,128,512]{2,1,0:T(8,128)(2,1)}, u32[]{:S(2)}) copy-start(bf16[2,128,512]{2,1,0:T(8,128)(2,1)} %wdn_ref.1) | copy-start | bytes 786436
  74.9 2.5 %copy-start.4 = (bf16[2,128,512]{2,1,0:T(8,128)(2,1)S(1)}, bf16[2,128,512]{2,1,0:T(8,128)(2,1)}, u32[]{:S(2)}) copy-start(bf16[2,128,512]{2,1,0:T(8,128)(2,1)} %param.23) | copy-start | bytes 786436
  74.9 2.5 %copy-start.5 = (bf16[2,128,512]{2,1,0:T(8,128)(2,1)S(1)}, bf16[2,128,512]{2,1,0:T(8,128)(2,1)}, u32[]{:S(2)}) copy-start(bf16[2,128,512]{2,1,0:T(8,128)(2,1)} %param.22) | copy-start | bytes 786436
  74.9 2.5 %copy-start.6 = (bf16[2,128,512]{2,1,0:T(8,128)(2,1)S(1)}, bf16[2,128,512]{2,1,0:T(8,128)(2,1)}, u32[]{:S(2)}) copy-start(bf16[2,128,512]{2,1,0:T(8,128)(2,1)} %get-tuple-element.12) | copy-start | bytes 786436
  77.4 1.5 %copy-start.7 = (f32[16,128]{1,0:T(8,128)S(1)}, f32[16,128]{1,0:T(8,128)}, u32[]{:S(2)}) copy-start(f32[16,128]{1,0:T(8,128)} %get-tuple-element.10) | copy-start | bytes 24580
